TPU v7x, 32 devices: a whole 2x2x4 slice. The times are simulated.
32 devices in a mesh: dp: 8 (over y, x, core), fsdp: 4 (over z).
Axes of the slice: x: 2, y: 2, z: 4, core: 2. Of those that a mesh axis runs over, the one named last changes fastest.
Arguments:
- tokens: bfloat16 [32, 1024, 768], P(('dp', 'fsdp')), may hold values from -6 to 6
- cotangent: bfloat16 [32, 1024, 768], P(('dp', 'fsdp')), may hold values from -6 to 6
- lengths: int32 [32], P(('dp', 'fsdp')), may hold values from 64 to 1024, as said below
- inward_weight: float32 [768, 2304], P('fsdp'), may hold values from -0.21875 to 0.21875
- inward_moment: float32 [768, 2304], P('fsdp'), may hold values from -640 to 640
- inward_square: float32 [768, 2304], P('fsdp'), may hold values from 12544 to 50176
- outward_weight: float32 [768, 768], P('fsdp'), may hold values from -3.5 to 3.5
- outward_moment: float32 [768, 768], P('fsdp'), may hold values from -40 to 40
- outward_square: float32 [768, 768], P('fsdp'), may hold values from 49 to 196
- expand_weight: float32 [768, 3072], P('fsdp'), may hold values from -0.21875 to 0.21875
- expand_moment: float32 [768, 3072], P('fsdp'), may hold values from -320 to 320
- expand_square: float32 [768, 3072], P('fsdp'), may hold values from 2508 to 10035
- shrink_weight: float32 [3072, 768], P('fsdp'), may hold values from -0.109375 to 0.109375
- shrink_moment: float32 [3072, 768], P('fsdp'), may hold values from -512 to 512
- shrink_square: float32 [3072, 768], P('fsdp'), may hold values from 6272 to 25088
- vectors: float32 [13, 768], P(None, 'fsdp'), may hold values from -2 to 2
- vector_moment: float32 [13, 768], P(None, 'fsdp'), may hold values from -640 to 640
- vector_square: float32 [13, 768], P(None, 'fsdp'), may hold values from 12544 to 50176
Outputs:
- layer_output: bfloat16 [32, 1024, 768], P(('dp', 'fsdp'))
- token_gradient: bfloat16 [32, 1024, 768], P(('dp', 'fsdp'))
- inward_master: float32 [768, 2304], P('fsdp')
- inward_momentum: float32 [768, 2304], P('fsdp')
- inward_squares: float32 [768, 2304], P('fsdp')
- outward_master: float32 [768, 768], P('fsdp')
- outward_momentum: float32 [768, 768], P('fsdp')
- outward_squares: float32 [768, 768], P('fsdp')
- expand_master: float32 [768, 3072], P('fsdp')
- expand_momentum: float32 [768, 3072], P('fsdp')
- expand_squares: float32 [768, 3072], P('fsdp')
- shrink_master: float32 [3072, 768], P('fsdp')
- shrink_momentum: float32 [3072, 768], P('fsdp')
- shrink_squares: float32 [3072, 768], P('fsdp')
- vector_master: float32 [13, 768], P(None, 'fsdp')
- vector_momentum: float32 [13, 768], P(None, 'fsdp')
- vector_squares: float32 [13, 768], P(None, 'fsdp')
Inputs may be any that keep to these rules, and one draw needn't show every extreme that they name: Row r holds one sequence in positions 0 to lengths[r] - 1 and padding after it; some row has exactly 1024.
All inputs are finite; a program needn't handle non-finite values.
Results may differ from a plain program's by a relative error of at most 0.015.
The roundings to bfloat16 on the way count: a program that leaves them out, or rounds other values in their place, can miss the bound.
Values may be sent and summed in bfloat16 or wider, within the bound.
No kernel may reach another device: no remote copies, remote signals or barrier semaphores. Data moves between devices by JAX's collectives and lax.ppermute only.
A program may use at most 256 MiB of HBM per device.

v0:
```python
import math

import jax
import jax.numpy as jnp
from jax import lax
from jax.sharding import PartitionSpec as P

D = 768
HEADS = 12
HEAD = 64
FF = 3072
QBLOCK = 512
STEP = 10
OUT_FAN = 3


NEG_FILL = -1000000000.0
NORM_EPS = 1e-12
BETA_ONE = 0.5
BETA_TWO = 0.5
ADAM_EPS = 1e-08
WEIGHT_DECAY = 0.01
ROOT_HALF = 0.7071067811865476
INV_ROOT_TAU = 0.3989422804014327


def rotary_tables(length, head_size, head_count):
    column = jnp.arange(head_size * head_count) % head_size // 2
    freqs = jnp.power(10000.0, column.astype(jnp.float32) * (-2.0 / head_size))
    angles = jnp.arange(length, dtype=jnp.float32)[:, None] * freqs[None, :]
    return (jnp.cos(angles), jnp.sin(angles))


def turn(values, cosine_table, sine_table):
    parity = jnp.arange(values.shape[-1]) % 2 == 0
    shifted_up = jnp.roll(values, -1, axis=-1)
    shifted_down = jnp.roll(values, 1, axis=-1)
    return values * cosine_table + jnp.where(parity, -shifted_up, shifted_down) * sine_table


def turn_back(incoming, cosine_table, sine_table):
    parity = jnp.arange(incoming.shape[-1]) % 2 == 0
    shifted_up = jnp.roll(incoming, -1, axis=-1)
    shifted_down = jnp.roll(incoming, 1, axis=-1)
    return incoming * cosine_table + jnp.where(parity, shifted_up, -shifted_down) * sine_table


def norm_forward(summed, gain_vec, shift_vec):
    center = summed - jnp.mean(summed, -1, keepdims=True)
    inverse = lax.rsqrt(jnp.mean(center * center, -1, keepdims=True) + NORM_EPS)
    normed = center * inverse
    return (normed * gain_vec + shift_vec, normed, inverse)


def norm_backward(incoming, normed, inverse, gain_vec):
    scaled = incoming * gain_vec
    result = inverse * (
        scaled
        - jnp.mean(scaled, -1, keepdims=True)
        - normed * jnp.mean(scaled * normed, -1, keepdims=True)
    )
    return (result, jnp.sum(incoming * normed, 0), jnp.sum(incoming, 0))


def gelu_slope(hidden):
    return (
        0.5 * (1.0 + lax.erf(hidden * ROOT_HALF))
        + hidden * jnp.exp(-0.5 * hidden * hidden) * INV_ROOT_TAU
    )


def attend_block(query_blk, key_heads, value_heads, usable_row, score_scale):
    scores = (
        jnp.einsum("qhd,khd->hqk", query_blk, key_heads, preferred_element_type=jnp.float32)
        * score_scale
    )
    scores = jnp.where(usable_row[None, None, :], scores, NEG_FILL)
    top_score = jnp.max(scores, -1, keepdims=True)
    expons = jnp.exp(scores - top_score)
    totals = jnp.sum(expons, -1, keepdims=True)
    weights = (expons / totals).astype(jnp.bfloat16)
    mixed_out = jnp.einsum("hqk,khd->qhd", weights, value_heads, preferred_element_type=jnp.float32)
    return (mixed_out.astype(jnp.bfloat16), (top_score + jnp.log(totals))[..., 0])


def attend_back_block(running, pieces, key_heads, value_heads, usable_row, score_scale):
    key_acc, value_acc = running
    query_blk, incoming_blk, logsum_blk = pieces
    scores = (
        jnp.einsum("qhd,khd->hqk", query_blk, key_heads, preferred_element_type=jnp.float32)
        * score_scale
    )
    scores = jnp.where(usable_row[None, None, :], scores, NEG_FILL)
    probs_full = jnp.exp(scores - logsum_blk[..., None])
    probs_low = probs_full.astype(jnp.bfloat16)
    prob_back = jnp.einsum(
        "qhd,khd->hqk", incoming_blk, value_heads, preferred_element_type=jnp.float32
    )
    row_dot = jnp.sum(probs_full * prob_back, -1, keepdims=True)
    score_back = (probs_full * (prob_back - row_dot)).astype(jnp.bfloat16)
    query_back = (
        jnp.einsum("hqk,khd->qhd", score_back, key_heads, preferred_element_type=jnp.float32)
        * score_scale
    )
    key_acc = (
        key_acc
        + jnp.einsum("hqk,qhd->khd", score_back, query_blk, preferred_element_type=jnp.float32)
        * score_scale
    )
    value_acc = value_acc + jnp.einsum(
        "hqk,qhd->khd", probs_low, incoming_blk, preferred_element_type=jnp.float32
    )
    return ((key_acc, value_acc), query_back)


def adam_update(master, moment, square, gradient, rate, decay):
    momentum = BETA_ONE * moment + (1.0 - BETA_ONE) * gradient
    squares = BETA_TWO * square + (1.0 - BETA_TWO) * gradient * gradient
    corrected = momentum / (1.0 - BETA_ONE**STEP)
    spread = jnp.sqrt(squares / (1.0 - BETA_TWO**STEP))
    return (master - rate * (corrected / (spread + ADAM_EPS) + decay * master), momentum, squares)


def local(
    tokens,
    cotangent,
    lengths,
    inward_weight,
    inward_moment,
    inward_square,
    outward_weight,
    outward_moment,
    outward_square,
    expand_weight,
    expand_moment,
    expand_square,
    shrink_weight,
    shrink_moment,
    shrink_square,
    vectors,
    vector_moment,
    vector_square,
):
    row_count, length, model_width = tokens.shape
    blocks = length // QBLOCK
    score_scale = 1.0 / math.sqrt(HEAD)
    shards = (
        inward_weight.astype(jnp.bfloat16),
        outward_weight.astype(jnp.bfloat16),
        expand_weight.astype(jnp.bfloat16),
        shrink_weight.astype(jnp.bfloat16),
        vectors.astype(jnp.bfloat16),
    )
    inward_full, outward_full, expand_full, shrink_full, vector_full = (
        lax.all_gather(shards[0], "fsdp", axis=0, tiled=True),
        lax.all_gather(shards[1], "fsdp", axis=0, tiled=True),
        lax.all_gather(shards[2], "fsdp", axis=0, tiled=True),
        lax.all_gather(shards[3], "fsdp", axis=0, tiled=True),
        lax.all_gather(shards[4], "fsdp", axis=1, tiled=True),
    )
    vector_vals = vector_full.astype(jnp.float32)
    cosine_table, sine_table = rotary_tables(length, HEAD, HEADS)
    usable = jnp.arange(length)[None, :] < lengths[:, None]
    flat_tokens = tokens.reshape(-1, model_width)
    joint_proj = jnp.dot(
        flat_tokens, inward_full, preferred_element_type=jnp.float32
    ) + vector_vals[4:7].reshape(-1)
    joint_proj = joint_proj.reshape(row_count, length, 3 * model_width)
    queries = turn(joint_proj[..., :model_width], cosine_table, sine_table).astype(jnp.bfloat16)
    keys_all = turn(
        joint_proj[..., model_width : 2 * model_width], cosine_table, sine_table
    ).astype(jnp.bfloat16)
    values_all = joint_proj[..., 2 * model_width :].astype(jnp.bfloat16)

    def attend_row(pieces):
        query_row, key_row, value_row, usable_row = pieces
        query_blocks = query_row.reshape(blocks, QBLOCK, HEADS, HEAD)
        key_heads = key_row.reshape(length, HEADS, HEAD)
        value_heads = value_row.reshape(length, HEADS, HEAD)
        mixed_out, logsum = lax.map(
            lambda query_blk: attend_block(
                query_blk, key_heads, value_heads, usable_row, score_scale
            ),
            query_blocks,
        )
        return (mixed_out.reshape(length, model_width), logsum)

    attended, logsums = lax.map(attend_row, (queries, keys_all, values_all, usable))
    attended_flat = attended.reshape(-1, model_width)
    residual_one = flat_tokens.astype(jnp.float32) + (
        jnp.dot(attended_flat, outward_full, preferred_element_type=jnp.float32) + vector_vals[7]
    )
    first_out, normed_one, inverse_one = norm_forward(residual_one, vector_vals[0], vector_vals[2])
    first_low = first_out.astype(jnp.bfloat16)
    hidden = jnp.dot(first_low, expand_full, preferred_element_type=jnp.float32) + vector_vals[
        9:13
    ].reshape(-1)
    active = jax.nn.gelu(hidden, approximate=False).astype(jnp.bfloat16)
    residual_two = first_out + (
        jnp.dot(active, shrink_full, preferred_element_type=jnp.float32) + vector_vals[8]
    )
    final_out, normed_two, inverse_two = norm_forward(residual_two, vector_vals[1], vector_vals[3])
    layer_output = final_out.astype(jnp.bfloat16).reshape(row_count, length, model_width)
    inward_full, outward_full, expand_full, shrink_full, vector_full = (
        lax.all_gather(shards[0], "fsdp", axis=0, tiled=True),
        lax.all_gather(shards[1], "fsdp", axis=0, tiled=True),
        lax.all_gather(shards[2], "fsdp", axis=0, tiled=True),
        lax.all_gather(shards[3], "fsdp", axis=0, tiled=True),
        lax.all_gather(shards[4], "fsdp", axis=1, tiled=True),
    )
    vector_vals = vector_full.astype(jnp.float32)
    incoming = (cotangent.astype(jnp.float32) * usable[..., None]).reshape(-1, model_width)
    second_back, second_gain, second_shift = norm_backward(
        incoming, normed_two, inverse_two, vector_vals[1]
    )
    down_back = second_back.astype(jnp.bfloat16)
    down_bias = jnp.sum(down_back, 0, dtype=jnp.float32)
    shrink_grad = jnp.einsum("nf,nd->fd", active, down_back, preferred_element_type=jnp.float32)
    active_back = jnp.einsum(
        "nd,fd->nf", down_back, shrink_full, preferred_element_type=jnp.float32
    )
    hidden_back = (active_back * gelu_slope(hidden)).astype(jnp.bfloat16)
    hidden_bias = jnp.sum(hidden_back, 0, dtype=jnp.float32)
    expand_grad = jnp.einsum(
        "nd,nf->df", first_low, hidden_back, preferred_element_type=jnp.float32
    )
    first_back = second_back + jnp.einsum(
        "nf,df->nd", hidden_back, expand_full, preferred_element_type=jnp.float32
    )
    stream_back, first_gain, first_shift = norm_backward(
        first_back, normed_one, inverse_one, vector_vals[0]
    )
    branch_back = stream_back.astype(jnp.bfloat16)
    branch_bias = jnp.sum(branch_back, 0, dtype=jnp.float32)
    outward_grad = jnp.einsum(
        "nd,ne->de", attended_flat, branch_back, preferred_element_type=jnp.float32
    )
    mixed_back = jnp.einsum(
        "ne,de->nd", branch_back, outward_full, preferred_element_type=jnp.float32
    ).astype(jnp.bfloat16)

    def back_row(pieces):
        query_row, key_row, value_row, usable_row, logsum_row, incoming_row = pieces
        query_blocks = query_row.reshape(blocks, QBLOCK, HEADS, HEAD)
        incoming_blocks = incoming_row.reshape(blocks, QBLOCK, HEADS, HEAD)
        key_heads = key_row.reshape(length, HEADS, HEAD)
        value_heads = value_row.reshape(length, HEADS, HEAD)
        zero_acc = jnp.zeros((length, HEADS, HEAD), jnp.float32)
        (key_acc, value_acc), query_acc = lax.scan(
            lambda running, parts: attend_back_block(
                running, parts, key_heads, value_heads, usable_row, score_scale
            ),
            (zero_acc, zero_acc),
            (query_blocks, incoming_blocks, logsum_row),
        )
        return (
            query_acc.reshape(length, model_width),
            key_acc.reshape(length, model_width),
            value_acc.reshape(length, model_width),
        )

    query_back, key_back, value_back = lax.map(
        back_row,
        (
            queries,
            keys_all,
            values_all,
            usable,
            logsums,
            mixed_back.reshape(row_count, length, model_width),
        ),
    )
    joint_back = (
        jnp.concatenate(
            [
                turn_back(query_back, cosine_table, sine_table),
                turn_back(key_back, cosine_table, sine_table),
                value_back,
            ],
            -1,
        )
        .astype(jnp.bfloat16)
        .reshape(-1, 3 * model_width)
    )
    joint_bias = jnp.sum(joint_back, 0, dtype=jnp.float32)
    inward_grad = jnp.einsum(
        "nd,ne->de", flat_tokens, joint_back, preferred_element_type=jnp.float32
    )
    token_back = (
        stream_back
        + jnp.einsum("ne,de->nd", joint_back, inward_full, preferred_element_type=jnp.float32)
    ).astype(jnp.bfloat16)
    token_back = token_back.reshape(row_count, length, model_width)
    vector_grad = jnp.concatenate(
        [
            jnp.stack([first_gain, second_gain, first_shift, second_shift]),
            joint_bias.reshape(3, model_width),
            branch_bias[None, :],
            down_bias[None, :],
            hidden_bias.reshape(-1, model_width),
        ],
        0,
    )
    reduced = (
        lax.psum_scatter(
            inward_grad.astype(jnp.bfloat16), "fsdp", scatter_dimension=0, tiled=True
        ).astype(jnp.float32),
        lax.psum_scatter(
            outward_grad.astype(jnp.bfloat16), "fsdp", scatter_dimension=0, tiled=True
        ).astype(jnp.float32),
        lax.psum_scatter(
            expand_grad.astype(jnp.bfloat16), "fsdp", scatter_dimension=0, tiled=True
        ).astype(jnp.float32),
        lax.psum_scatter(
            shrink_grad.astype(jnp.bfloat16), "fsdp", scatter_dimension=0, tiled=True
        ).astype(jnp.float32),
        lax.psum_scatter(
            vector_grad.astype(jnp.bfloat16), "fsdp", scatter_dimension=1, tiled=True
        ).astype(jnp.float32),
    )
    inward_sum, outward_sum, expand_sum, shrink_sum, vector_sum = lax.psum(
        (reduced[0], reduced[1], reduced[2], reduced[3], reduced[4]), "dp"
    )
    inward_new = adam_update(
        inward_weight, inward_moment, inward_square, inward_sum, 1.0 / math.sqrt(D), WEIGHT_DECAY
    )
    outward_new = adam_update(
        outward_weight,
        outward_moment,
        outward_square,
        outward_sum,
        1.0 / math.sqrt(OUT_FAN),
        WEIGHT_DECAY,
    )
    expand_new = adam_update(
        expand_weight, expand_moment, expand_square, expand_sum, 1.0 / math.sqrt(D), WEIGHT_DECAY
    )
    shrink_new = adam_update(
        shrink_weight, shrink_moment, shrink_square, shrink_sum, 1.0 / math.sqrt(FF), WEIGHT_DECAY
    )
    vector_new = adam_update(vectors, vector_moment, vector_square, vector_sum, 0.5, 0.0)
    return (
        layer_output,
        token_back,
        inward_new[0],
        inward_new[1],
        inward_new[2],
        outward_new[0],
        outward_new[1],
        outward_new[2],
        expand_new[0],
        expand_new[1],
        expand_new[2],
        shrink_new[0],
        shrink_new[1],
        shrink_new[2],
        vector_new[0],
        vector_new[1],
        vector_new[2],
    )


def solution(mesh):
    in_specs = (
        P(("dp", "fsdp"), None, None),
        P(("dp", "fsdp"), None, None),
        P(("dp", "fsdp")),
        P("fsdp", None),
        P("fsdp", None),
        P("fsdp", None),
        P("fsdp", None),
        P("fsdp", None),
        P("fsdp", None),
        P("fsdp", None),
        P("fsdp", None),
        P("fsdp", None),
        P("fsdp", None),
        P("fsdp", None),
        P("fsdp", None),
        P(None, "fsdp"),
        P(None, "fsdp"),
        P(None, "fsdp"),
    )
    out_specs = (
        P(("dp", "fsdp"), None, None),
        P(("dp", "fsdp"), None, None),
        P("fsdp", None),
        P("fsdp", None),
        P("fsdp", None),
        P("fsdp", None),
        P("fsdp", None),
        P("fsdp", None),
        P("fsdp", None),
        P("fsdp", None),
        P("fsdp", None),
        P("fsdp", None),
        P("fsdp", None),
        P("fsdp", None),
        P(None, "fsdp"),
        P(None, "fsdp"),
        P(None, "fsdp"),
    )
    return jax.shard_map(local, mesh=mesh, in_specs=in_specs, out_specs=out_specs, check_vma=False)
```

profile of v0, /device:TPU:0, one launch (start us, length us, event | category | flops | bytes accessed | tf_op | source)
XLA Modules:
  0.0 1084.8 jit_solution(922068582932934968)
XLA Ops:
  15.1 14.9 %all-gather = bf16[4,192,13]{1,2,0:T(8,128)(2,1)S(1)} all-gather(bf16[1,192,13]{1,2,0:T(8,128)(2,1)S(1)} %convert_bitcast_fusion), channel_id=1, replica_groups=mesh['dp'=8,'fsdp'=4] {'fsdp'}, dimensions={0}, use_global_device_ids=true | all-gather | bytes 24960 | tf_op jit(solution)/shard_map/all_gather | solution.py:159
  36.5 46.6 %all-gather.6.cloned.1.call-done = bf16[768,2304]{1,0:T(8,128)(2,1)} async-done(((bf16[192,2304]{1,0:T(8,128)(2,1)}), bf16[768,2304]{1,0:T(8,128)(2,1)}) %all-gather.6.cloned.1.call-update) | async-done | bytes 3538960 | tf_op jit(solution)/shard_map/all_gather | solution.py:155
  83.1 5.8 add_bitcast_fusion
  94.7 10.4 fusion.115
  107.7 16.1 %fusion.56 = (bf16[1,1024,768]{2,1,0:T(8,128)(2,1)}, bf16[1,1024,768]{2,1,0:T(8,128)(2,1)}) fusion(f32[1,1024,2304]{2,1,0:T(8,128)} %copy-done.2, f32[1,1024,1]{2,1,0:T(8,128)} %get-tuple-element.432, f32[1,1024,767]{2,1,0:T(8,128)} %get-tuple-element.436, f32[1,1024,767]{2,1,0:T(8,128)S(1)} %get-tuple-element.435, f32[1,1024,1]{2,1,0:T(8,128)} %get-tuple-element.431, ...), kind=kLoop, calls=%fused_computation.89 | loop fusion | flops 13369344 | bytes 22023936 | tf_op jit(solution)/shard_map/convert_element_type | solution.py:172
  131.9 73.9 %while.48 = (s32[]{:T(128)}, bf16[2,512,12,64]{1,3,2,0:T(8,128)(2,1)}, f32[2,12,512]{2,1,0:T(8,128)S(1)}, bf16[2,512,12,64]{1,3,2,0:T(8,128)(2,1)}, bf16[1024,12...) while((s32[]{:T(128)}, ...), condition=%wide.region_3.4_spmd.clone, body=%wide.region_0.3_spmd.clone.sunk | while | flops 1686498304 | bytes 93040808 | solution.py:180
  133.0 11.8 %fusion.159 = (f32[12,512]{1,0:T(8,128)S(1)}, f32[12,512,1024]{2,1,0:T(8,128)}) fusion(pred[1024]{0:T(1024)(128)(4,1)S(1)} %iota_compare_fusion.5, bf16[1024,12,64]{0,2,1:T(8,128)(2,1)S(1)} %get-tuple-element.593, bf16[2,512,12,64]{1,3,2,0:T(8,128)(2,1)} %get-tuple-element.592, s32[]{:T(128)S(6)} %copy.156), kind=kOutput, calls=%fused_computation.5.clone.1 | convolution fusion | flops 824174592 | bytes 27550724 | tf_op jit(solution)/shard_map/while/body/eval_jaxpr/while/body/eval_jaxpr/qhd,khd->hqk/dot_general | solution.py:74
  144.8 11.4 %fusion.160 = f32[12,512]{1,0:T(8,128)S(1)} fusion(f32[12,512,1024]{2,1,0:T(8,128)} %get-tuple-element.559, f32[12,512]{1,0:T(8,128)S(1)} %get-tuple-element.560, pred[1024]{0:T(1024)(128)(4,1)S(1)} %iota_compare_fusion.5), kind=kLoop, calls=%fused_computation.6.clone.1 | loop fusion | flops 25159680 | bytes 25216000 | tf_op jit(solution)/shard_map/while/body/eval_jaxpr/while/body/eval_jaxpr/reduce_sum | solution.py:80
  156.2 11.8 %fusion.161 = bf16[2,512,12,64]{1,3,2,0:T(8,128)(2,1)S(1)} fusion(bf16[2,512,12,64]{1,3,2,0:T(8,128)(2,1)S(1)} %copy-done.38, s32[]{:T(128)S(6)} %copy.156, bf16[1024,12,64]{0,2,1:T(8,128)(2,1)} %get-tuple-element.594, f32[12,512,1024]{2,1,0:T(8,128)} %get-tuple-element.559, f32[12,512]{1,0:T(8,128)S(1)} %fusion.160, ...), kind=kOutput, calls=%fused_computation.10.clone.1 | convolution fusion | flops 837156864 | bytes 27591684 | tf_op jit(solution)/shard_map/while/body/eval_jaxpr/while/body/eval_jaxpr/hqk,khd->qhd/dot_general | solution.py:82
  169.8 11.8 %fusion.159 = (f32[12,512]{1,0:T(8,128)S(1)}, f32[12,512,1024]{2,1,0:T(8,128)}) fusion(pred[1024]{0:T(1024)(128)(4,1)S(1)} %iota_compare_fusion.5, bf16[1024,12,64]{0,2,1:T(8,128)(2,1)S(1)} %get-tuple-element.593, bf16[2,512,12,64]{1,3,2,0:T(8,128)(2,1)} %get-tuple-element.592, s32[]{:T(128)S(6)} %copy.156), kind=kOutput, calls=%fused_computation.5.clone.1 | convolution fusion | flops 824174592 | bytes 27550724 | tf_op jit(solution)/shard_map/while/body/eval_jaxpr/while/body/eval_jaxpr/qhd,khd->hqk/dot_general | solution.py:74
  181.6 11.3 %fusion.160 = f32[12,512]{1,0:T(8,128)S(1)} fusion(f32[12,512,1024]{2,1,0:T(8,128)} %get-tuple-element.559, f32[12,512]{1,0:T(8,128)S(1)} %get-tuple-element.560, pred[1024]{0:T(1024)(128)(4,1)S(1)} %iota_compare_fusion.5), kind=kLoop, calls=%fused_computation.6.clone.1 | loop fusion | flops 25159680 | bytes 25216000 | tf_op jit(solution)/shard_map/while/body/eval_jaxpr/while/body/eval_jaxpr/reduce_sum | solution.py:80
  193.0 11.7 %fusion.161 = bf16[2,512,12,64]{1,3,2,0:T(8,128)(2,1)S(1)} fusion(bf16[2,512,12,64]{1,3,2,0:T(8,128)(2,1)S(1)} %copy-done.38, s32[]{:T(128)S(6)} %copy.156, bf16[1024,12,64]{0,2,1:T(8,128)(2,1)} %get-tuple-element.594, f32[12,512,1024]{2,1,0:T(8,128)} %get-tuple-element.559, f32[12,512]{1,0:T(8,128)S(1)} %fusion.160, ...), kind=kOutput, calls=%fused_computation.10.clone.1 | convolution fusion | flops 837156864 | bytes 27591684 | tf_op jit(solution)/shard_map/while/body/eval_jaxpr/while/body/eval_jaxpr/hqk,khd->qhd/dot_general | solution.py:82
  215.5 39.2 %fusion.40 = (bf16[1024,3072]{1,0:T(8,128)(2,1)}, f32[1024,3072]{1,0:T(8,128)}) fusion(f32[3072]{0:T(1024)S(1)} %copy-done.59, bf16[768,3072]{1,0:T(8,128)(2,1)} %all-gather.10.cloned.1.call-done, f32[1024,768]{0,1:T(8,128)} %copy-done.7, f32[768]{0:T(1024)S(1)} %copy-done.66, f32[768]{0:T(1024)S(1)} %copy-done.55, f32[1024]{0:T(1024)S(1)} %add_rsqrt_fusion.1, ...), kind=kOutput, calls=%fused_computation.50 | convolution fusion | flops 5043388416 | bytes 26765312 | tf_op jit(solution)/shard_map/dot_general | solution.py:195
  254.7 40.4 %all-gather.12.cloned.1.call-done = bf16[3072,768]{1,0:T(8,128)(2,1)} async-done(((bf16[768,768]{1,0:T(8,128)(2,1)}), bf16[3072,768]{1,0:T(8,128)(2,1)}) %all-gather.12.cloned.1.call-update) | async-done | bytes 4718608 | tf_op jit(solution)/shard_map/all_gather | solution.py:158
  295.1 9.4 fusion.117
  311.1 14.7 %fusion.118 = (bf16[3072]{0:T(1024)(128)(2,1)}, bf16[1024,3072]{1,0:T(8,128)(2,1)}) fusion(f32[1024,3072]{1,0:T(8,128)} %get-tuple-element.453, f32[3072]{0:T(1024)S(1)} %copy-done.59, bf16[1024,768]{0,1:T(8,128)(2,1)S(1)} %get-tuple-element.422, bf16[3072,768]{1,0:T(8,128)(2,1)S(1)} %bitcast.197), kind=kOutput, calls=%fused_computation.215 | convolution fusion | flops 4869583872 | bytes 25184256 | tf_op jit(solution)/shard_map/nd,fd->nf/dot_general | solution.py:219
  325.8 9.9 multiply_reduce_fusion.1
  348.7 228.0 %while.49 = (s32[]{:T(128)}, f32[1024,12,64]{0,2,1:T(8,128)}, f32[1024,12,64]{0,2,1:T(8,128)}, f32[2,512,12,64]{1,0,3,2:T(2,128)}, bf16[2,512,12,64]{1,3,2,0:T(8...) while((s32[]{:T(128)}, f32[1024,12,64]{0,2,1:T(8,128)}, ...), condition=%wide.region_14.15_spmd.clone, body=%wide.region_12.14_spmd.clone.sunk | while | flops 4125223936 | bytes 223522992 | solution.py:249
  349.5 11.4 %fusion.171 = f32[12,512,1024]{2,1,0:T(8,128)} fusion(bf16[1024,12,64]{0,2,1:T(8,128)(2,1)S(1)} %get-tuple-element.626, bf16[2,512,12,64]{1,3,2,0:T(8,128)(2,1)} %get-tuple-element.625, s32[]{:T(128)S(6)} %copy.166), kind=kOutput, calls=%fused_computation.32.clone.1 | convolution fusion | flops 805306368 | bytes 27525124 | tf_op jit(solution)/shard_map/while/body/eval_jaxpr/while/body/eval_jaxpr/qhd,khd->hqk/dot_general | solution.py:90
  360.9 13.1 %bitcast_add_fusion.5 = f32[1024,12,64]{0,2,1:T(8,128)} fusion(f32[1024,12,64]{0,2,1:T(8,128)} %get-tuple-element.611, f32[12,512,1024]{2,1,0:T(8,128)} %fusion.171, f32[12,512]{1,0:T(8,128)S(1)} %dynamic-slice_bitcast_fusion.2, pred[1024]{0:T(1024)(128)(4,1)S(1)} %iota_compare_fusion.6, pred[]{:T(512)S(6)} %compare.12, ...), kind=kOutput, calls=%fused_computation.25.clone.1 | convolution fusion | flops 832045056 | bytes 32269316 | tf_op jit(solution)/shard_map/while/body/eval_jaxpr/while/body/eval_jaxpr/hqk,qhd->khd/dot_general | solution.py:110
  374.0 17.4 %multiply_reduce_fusion.8 = (f32[12,512]{1,0:T(8,128)S(1)}, f32[12,512,1024]{2,1,0:T(8,128)}) fusion(f32[12,512,1024]{2,1,0:T(8,128)} %fusion.171, f32[12,512]{1,0:T(8,128)S(1)} %dynamic-slice_bitcast_fusion.2, pred[1024]{0:T(1024)(128)(4,1)S(1)} %iota_compare_fusion.6, bf16[1024,12,64]{0,2,1:T(8,128)(2,1)} %get-tuple-element.629, ...), kind=kOutput, calls=%fused_computation.20.clone.1 | convolution fusion | flops 836757504 | bytes 52741124 | tf_op jit(solution)/shard_map/while/body/eval_jaxpr/while/body/eval_jaxpr/qhd,khd->hqk/dot_general | solution.py:96
  391.5 21.4 %multiply_convert_fusion.2 = bf16[12,512,1024]{2,1,0:T(8,128)(2,1)} fusion(f32[12,512,1024]{2,1,0:T(8,128)} %get-tuple-element.571, f32[12,512,1024]{2,1,0:T(8,128)} %fusion.171, f32[12,512]{1,0:T(8,128)S(1)} %get-tuple-element.572, f32[12,512]{1,0:T(8,128)S(1)} %dynamic-slice_bitcast_fusion.2, pred[1024]{0:T(1024)(128)(4,1)S(1)} %iota_compare_fusion.6), kind=kLoop, calls=%fused_computation.19.clone.1 | loop fusion | flops 37748736 | bytes 62964736 | tf_op jit(solution)/shard_map/while/body/eval_jaxpr/while/body/eval_jaxpr/convert_element_type | solution.py:100
  412.9 9.6 multiply_bitcast_fusion.2
  422.6 8.9 bitcast_add_fusion.4
  433.1 28.7 %dynamic_update_slice.35 = f32[2,512,12,64]{1,0,3,2:T(2,128)} dynamic-update-slice(f32[2,512,12,64]{1,0,3,2:T(2,128)} %get-tuple-element.612, f32[1,512,12,64]{1,0,3,2:T(1,128)S(1)} %copy.149, s32[]{:T(128)S(6)} %copy.166, s32[]{:T(128)} %constant.118.clone.1..sunk, s32[]{:T(128)} %constant.118.clone.1..sunk, s32[]{:T(128)} %constant.118.clone.1..sunk) | dynamic-update-slice | bytes 3145732 | tf_op jit(solution)/shard_map/while/body/eval_jaxpr/while/body/jit(dynamic_update_index_in_dim)/dynamic_update_slice | solution.py:249
  462.5 11.4 %fusion.171 = f32[12,512,1024]{2,1,0:T(8,128)} fusion(bf16[1024,12,64]{0,2,1:T(8,128)(2,1)S(1)} %get-tuple-element.626, bf16[2,512,12,64]{1,3,2,0:T(8,128)(2,1)} %get-tuple-element.625, s32[]{:T(128)S(6)} %copy.166), kind=kOutput, calls=%fused_computation.32.clone.1 | convolution fusion | flops 805306368 | bytes 27525124 | tf_op jit(solution)/shard_map/while/body/eval_jaxpr/while/body/eval_jaxpr/qhd,khd->hqk/dot_general | solution.py:90
  473.8 14.0 %bitcast_add_fusion.5 = f32[1024,12,64]{0,2,1:T(8,128)} fusion(f32[1024,12,64]{0,2,1:T(8,128)} %get-tuple-element.611, f32[12,512,1024]{2,1,0:T(8,128)} %fusion.171, f32[12,512]{1,0:T(8,128)S(1)} %dynamic-slice_bitcast_fusion.2, pred[1024]{0:T(1024)(128)(4,1)S(1)} %iota_compare_fusion.6, pred[]{:T(512)S(6)} %compare.12, ...), kind=kOutput, calls=%fused_computation.25.clone.1 | convolution fusion | flops 832045056 | bytes 32269316 | tf_op jit(solution)/shard_map/while/body/eval_jaxpr/while/body/eval_jaxpr/hqk,qhd->khd/dot_general | solution.py:110
  487.9 17.4 %multiply_reduce_fusion.8 = (f32[12,512]{1,0:T(8,128)S(1)}, f32[12,512,1024]{2,1,0:T(8,128)}) fusion(f32[12,512,1024]{2,1,0:T(8,128)} %fusion.171, f32[12,512]{1,0:T(8,128)S(1)} %dynamic-slice_bitcast_fusion.2, pred[1024]{0:T(1024)(128)(4,1)S(1)} %iota_compare_fusion.6, bf16[1024,12,64]{0,2,1:T(8,128)(2,1)} %get-tuple-element.629, ...), kind=kOutput, calls=%fused_computation.20.clone.1 | convolution fusion | flops 836757504 | bytes 52741124 | tf_op jit(solution)/shard_map/while/body/eval_jaxpr/while/body/eval_jaxpr/qhd,khd->hqk/dot_general | solution.py:96
  505.3 21.4 %multiply_convert_fusion.2 = bf16[12,512,1024]{2,1,0:T(8,128)(2,1)} fusion(f32[12,512,1024]{2,1,0:T(8,128)} %get-tuple-element.571, f32[12,512,1024]{2,1,0:T(8,128)} %fusion.171, f32[12,512]{1,0:T(8,128)S(1)} %get-tuple-element.572, f32[12,512]{1,0:T(8,128)S(1)} %dynamic-slice_bitcast_fusion.2, pred[1024]{0:T(1024)(128)(4,1)S(1)} %iota_compare_fusion.6), kind=kLoop, calls=%fused_computation.19.clone.1 | loop fusion | flops 37748736 | bytes 62964736 | tf_op jit(solution)/shard_map/while/body/eval_jaxpr/while/body/eval_jaxpr/convert_element_type | solution.py:100
  526.7 9.6 multiply_bitcast_fusion.2
  536.4 9.8 bitcast_add_fusion.4
  547.8 28.7 %dynamic_update_slice.35 = f32[2,512,12,64]{1,0,3,2:T(2,128)} dynamic-update-slice(f32[2,512,12,64]{1,0,3,2:T(2,128)} %get-tuple-element.612, f32[1,512,12,64]{1,0,3,2:T(1,128)S(1)} %copy.149, s32[]{:T(128)S(6)} %copy.166, s32[]{:T(128)} %constant.118.clone.1..sunk, s32[]{:T(128)} %constant.118.clone.1..sunk, s32[]{:T(128)} %constant.118.clone.1..sunk) | dynamic-update-slice | bytes 3145732 | tf_op jit(solution)/shard_map/while/body/eval_jaxpr/while/body/jit(dynamic_update_index_in_dim)/dynamic_update_slice | solution.py:249
  576.7 4.3 broadcast_in_dim.104
  582.7 7.0 slice_bitcast_fusion.2
  598.8 18.3 %fusion.65 = (bf16[1024,768]{0,1:T(8,128)(2,1)S(1)}, bf16[1024,768]{0,1:T(8,128)(2,1)S(1)}) fusion(f32[1024,1]{0,1:T(1,128)S(1)} %get-tuple-element.441, f32[1024,767]{0,1:T(8,128)S(1)} %copy-done.11, f32[1024,767]{0,1:T(8,128)S(1)} %copy-done.10, f32[1024,1]{0,1:T(1,128)S(1)} %get-tuple-element.440, f32[1024,768]{0,1:T(8,128)S(1)} %bitcast.182, ...), kind=kLoop, calls=%fused_computation.102 | loop fusion | flops 13369344 | bytes 22023936 | tf_op jit(solution)/shard_map/convert.16
  620.5 4.9 convolution_convert_fusion.4
  625.6 7.5 fusion.54
  633.0 5.8 copy.128
  640.3 10.1 convolution_convert_fusion
  652.3 9.8 convolution_convert_fusion.1
  665.1 8.9 fusion.83
  678.2 58.0 %reduce-scatter.16.cloned.1.call-done = bf16[192,2304]{1,0:T(8,128)(2,1)} async-done(((bf16[768,2304]{1,0:T(8,128)(2,1)}), bf16[192,2304]{1,0:T(8,128)(2,1)}) %reduce-scatter.16.cloned.1.call-update) | async-done | bytes 884752 | tf_op jit(solution)/shard_map/reduce_scatter | solution.py:305
  736.2 88.0 %reduce-scatter.14.cloned.1.call-done = bf16[768,768]{1,0:T(8,128)(2,1)} async-done(((bf16[3072,768]{1,0:T(8,128)(2,1)}), bf16[768,768]{1,0:T(8,128)(2,1)}) %reduce-scatter.14.cloned.1.call-update) | async-done | bytes 1179664 | tf_op jit(solution)/shard_map/reduce_scatter | solution.py:314
  824.2 88.2 %reduce-scatter.12.cloned.1.call-done = bf16[192,3072]{1,0:T(8,128)(2,1)} async-done(((bf16[768,3072]{1,0:T(8,128)(2,1)}), bf16[192,3072]{1,0:T(8,128)(2,1)}) %reduce-scatter.12.cloned.1.call-update) | async-done | bytes 1179664 | tf_op jit(solution)/shard_map/reduce_scatter | solution.py:311
  912.4 144.8 %all-reduce.2 = (f32[192,2304]{1,0:T(8,128)}, f32[192,768]{1,0:T(8,128)}, f32[192,3072]{1,0:T(8,128)}, f32[768,768]{1,0:T(8,128)}, f32[13,192]{1,0:T(8,128)}) all-reduce(bf16[192,2304]{1,0:T(8,128)(2,1)} %reduce-scatter.16.cloned.1.call-done, ...), channel_id=1, replica_groups=mesh['dp'=8,'fsdp'=4] {'dp'}, use_global_device_ids=true, to_apply=%region_16.17 | all-reduce | flops 1771968 | bytes 10631808 | tf_op jit(solution)/shard_map/psum | solution.py:321
  1061.4 5.0 multiply_subtract_fusion.2
  1067.5 4.6 multiply_subtract_fusion.1
  1073.9 4.2 multiply_subtract_fusion
  (264 shorter events, 98.6 us)
Async XLA Ops:
  7.2 75.9 %all-gather.6.cloned.1.call-start = ((), (), s32[]{:S(2)}) async-start(), calls=%async_computation.5 | async-start | bytes 4423680 | tf_op jit(solution)/shard_map/all_gather | solution.py:155
  9.9 199.4 %all-gather.8.cloned.1.call-start = ((), (), s32[]{:S(2)}) async-start(), calls=%async_computation.6 | async-start | bytes 1474560 | tf_op jit(solution)/shard_map/all_gather | solution.py:156
  10.7 204.7 %all-gather.10.cloned.1.call-start = ((), (), s32[]{:S(2)}) async-start(), calls=%async_computation.7 | async-start | bytes 5898240 | tf_op jit(solution)/shard_map/all_gather | solution.py:157
  12.0 20.1 %copy-start.35 = (bf16[1,1024,768]{2,1,0:T(8,128)(2,1)S(1)}, bf16[1,1024,768]{2,1,0:T(8,128)(2,1)}, u32[]{:S(2)}) copy-start(bf16[1,1024,768]{2,1,0:T(8,128)(2,1)} %param.23) | copy-start | bytes 4718596
  12.0 283.1 %all-gather.12.cloned.1.call-start = ((), (), s32[]{:S(2)}) async-start(), calls=%async_computation.8 | async-start | bytes 5898240 | tf_op jit(solution)/shard_map/all_gather | solution.py:158
  15.0 661.7 %reduce-scatter.18.cloned.1.call-start = ((), (), s32[]{:S(2)}) async-start(), calls=%async_computation.13 | async-start | bytes 245760
  15.0 92.7 %copy-start.64 = (pred[768]{0:T(1024)(128)(4,1)}, pred[768]{0:T(1024)(128)(4,1)S(1)}, u32[]{:S(2)}) copy-start(pred[768]{0:T(1024)(128)(4,1)S(1)} %fusion.91) | copy-start | bytes 2308
  15.1 92.7 %copy-start.51 = (f32[768]{0:T(1024)}, f32[768]{0:T(1024)S(1)}, u32[]{:S(2)}) copy-start(f32[768]{0:T(1024)S(1)} %fusion.90) | copy-start | bytes 9220
  31.5 5.0 copy-start.46
  32.9 56.1 %copy-start.4 = (bf16[1,1024,768]{1,2,0:T(8,128)(2,1)}, bf16[1,1024,768]{1,2,0:T(8,128)(2,1)S(1)}, u32[]{:S(2)}) copy-start(bf16[1,1024,768]{1,2,0:T(8,128)(2,1)S(1)} %copy.114) | copy-start | bytes 4718596
  32.9 50.2 %copy-start.36 = (bf16[1,1024,768]{2,1,0:T(8,128)(2,1)S(1)}, bf16[1,1024,768]{2,1,0:T(8,128)(2,1)}, u32[]{:S(2)}) copy-start(bf16[1,1024,768]{2,1,0:T(8,128)(2,1)} %param.22) | copy-start | bytes 4718596
  89.0 4.1 copy-start.2
  144.8 11.4 %copy-start.38 = (bf16[2,512,12,64]{1,3,2,0:T(8,128)(2,1)S(1)}, bf16[2,512,12,64]{1,3,2,0:T(8,128)(2,1)}, u32[]{:S(2)}) copy-start(bf16[2,512,12,64]{1,3,2,0:T(8,128)(2,1)} %get-tuple-element.582) | copy-start | bytes 4718596 | tf_op jit(solution)/shard_map/while/body/eval_jaxpr/while
  181.6 11.3 %copy-start.38 = (bf16[2,512,12,64]{1,3,2,0:T(8,128)(2,1)S(1)}, bf16[2,512,12,64]{1,3,2,0:T(8,128)(2,1)}, u32[]{:S(2)}) copy-start(bf16[2,512,12,64]{1,3,2,0:T(8,128)(2,1)} %get-tuple-element.582) | copy-start | bytes 4718596 | tf_op jit(solution)/shard_map/while/body/eval_jaxpr/while
  213.3 122.4 %copy-start.48 = (f32[1024]{0:T(1024)}, f32[1024]{0:T(1024)S(1)}, u32[]{:S(2)}) copy-start(f32[1024]{0:T(1024)S(1)} %broadcast_multiply_fusion.5) | copy-start | bytes 12292
  215.4 120.3 %copy-start.53 = (f32[1024]{0:T(1024)}, f32[1024]{0:T(1024)S(1)}, u32[]{:S(2)}) copy-start(f32[1024]{0:T(1024)S(1)} %add_rsqrt_fusion.1) | copy-start | bytes 12292
  215.5 79.6 %copy-start.68 = (f32[768]{0:T(1024)S(1)}, f32[768]{0:T(1024)}, u32[]{:S(2)}) copy-start(f32[768]{0:T(1024)} %get-tuple-element.363) | copy-start | bytes 9220
  304.5 6.6 slice-start.2
  305.9 5.2 slice-start.3
  309.1 16.7 %slice-start = ((s8[4718592]{0:T(1024)(128)(4,1)}), s8[4194304]{0:T(1024)(128)(4,1)S(1)}, s32[]{:S(2)}) async-start(s8[4718592]{0:T(1024)(128)(4,1)} %bitcast.194), calls=%async_computation.14 | async-start | bytes 8388608
  311.1 14.7 %copy-start.40 = (bf16[1024,768]{0,1:T(8,128)(2,1)}, bf16[1024,768]{0,1:T(8,128)(2,1)S(1)}, u32[]{:S(2)}) copy-start(bf16[1024,768]{0,1:T(8,128)(2,1)S(1)} %get-tuple-element.422) | copy-start | bytes 4718596
  311.1 14.7 %copy-start.8 = (f32[1024,768]{0,1:T(8,128)S(1)}, f32[1024,768]{0,1:T(8,128)}, u32[]{:S(2)}) copy-start(f32[1024,768]{0,1:T(8,128)} %copy-done.7) | copy-start | bytes 9437188
  311.1 14.7 %slice-start.1 = ((s8[4718592]{0:T(1024)(128)(4,1)}), s8[524288]{0:T(1024)(128)(4,1)S(1)}, s32[]{:S(2)}) async-start(s8[4718592]{0:T(1024)(128)(4,1)} %bitcast.194), calls=%async_computation.15 | async-start | bytes 1048576
  422.6 9.0 copy-start.1
  536.4 9.8 copy-start.1
  582.7 7.0 copy-start
  595.4 21.7 %copy-start.16 = (bf16[1024,12,64]{0,2,1:T(8,128)(2,1)}, bf16[1024,12,64]{0,2,1:T(8,128)(2,1)S(1)}, u32[]{:S(2)}) copy-start(bf16[1024,12,64]{0,2,1:T(8,128)(2,1)S(1)} %convert.48) | copy-start | bytes 4718596
  620.4 5.1 copy-start.17
  620.5 5.1 copy-start.22
  620.5 57.7 %reduce-scatter.10.cloned.1.call-start = ((), (), s32[]{:S(2)}) async-start(), calls=%async_computation.9 | async-start | bytes 1474560 | tf_op jit(solution)/shard_map/reduce_scatter | solution.py:308
  625.5 110.7 %reduce-scatter.16.cloned.1.call-start = ((), (), s32[]{:S(2)}) async-start(), calls=%async_computation.12 | async-start | bytes 4423680 | tf_op jit(solution)/shard_map/reduce_scatter | solution.py:305
  638.9 185.3 %reduce-scatter.14.cloned.1.call-start = ((), (), s32[]{:S(2)}) async-start(), calls=%async_computation.11 | async-start | bytes 5898240 | tf_op jit(solution)/shard_map/reduce_scatter | solution.py:314
  650.4 262.0 %reduce-scatter.12.cloned.1.call-start = ((), (), s32[]{:S(2)}) async-start(), calls=%async_computation.10 | async-start | bytes 5898240 | tf_op jit(solution)/shard_map/reduce_scatter | solution.py:311
  674.0 383.2 %copy-start.45 = (f32[13,192]{1,0:T(8,128)S(1)}, f32[13,192]{1,0:T(8,128)}, u32[]{:S(2)}) copy-start(f32[13,192]{1,0:T(8,128)} %param.37) | copy-start | bytes 29956
  674.0 384.7 %copy-start.26 = (f32[192,768]{1,0:T(8,128)S(1)}, f32[192,768]{1,0:T(8,128)}, u32[]{:S(2)}) copy-start(f32[192,768]{1,0:T(8,128)} %param.28) | copy-start | bytes 1769476
  674.0 384.7 %copy-start.42 = (f32[192,768]{1,0:T(8,128)S(1)}, f32[192,768]{1,0:T(8,128)}, u32[]{:S(2)}) copy-start(f32[192,768]{1,0:T(8,128)} %param.29) | copy-start | bytes 1769476
  674.0 384.8 %copy-start.43 = (f32[192,768]{1,0:T(8,128)S(1)}, f32[192,768]{1,0:T(8,128)}, u32[]{:S(2)}) copy-start(f32[192,768]{1,0:T(8,128)} %param.30) | copy-start | bytes 1769476
  678.2 383.1 %copy-start.15 = (f32[192,2304]{1,0:T(8,128)S(1)}, f32[192,2304]{1,0:T(8,128)}, u32[]{:S(2)}) copy-start(f32[192,2304]{1,0:T(8,128)} %param.25) | copy-start | bytes 5308420
  1057.2 4.1 copy-start.33
  1057.2 4.1 copy-start.34
  1061.3 5.1 copy-start.13
  1061.3 5.0 copy-start.27
  1061.3 5.0 copy-start.28
  1061.3 6.2 copy-start.32
  1067.5 4.6 copy-start.14
  1067.5 4.6 copy-start.29
  1067.5 5.6 copy-start.30
  1067.5 6.3 copy-start.31
  (41 other events, 95.7 us)
Sparse Core Ops, SparseCore 0:
  10.2 72.8 all-gather.5
  85.3 29.1 all-gather.7
  116.6 88.5 all-gather.9
  207.2 87.8 all-gather.11
  620.6 17.7 reduce-scatter.17
  641.2 27.4 reduce-scatter.9
  671.1 65.0 reduce-scatter.15
  738.6 85.5 reduce-scatter.13
  826.6 85.7 reduce-scatter.11
where the time goes:
time: 1100 us; the launch traced here: 1080 us
  waiting for transfers between devices  321 us (29%)
  matrix products  297 us (27%)
  blocking collectives  160 us (15%)
  local copies, waits for them, and re-layouts  151 us (14%)
  other arithmetic  139 us (13%)
  between operations  15.5 us (1%)
    psum x1, blocking collectives, local(): lax.psum((reduced[0], reduced[1], reduced[2], reduced[3], reduced[4]), 'dp')  145 us
    reduce_scatter x1, waiting for transfers between devices, local(): lax.psum_scatter(expand_grad.astype(jnp.bfloat16), 'fsdp', scatter_dimens...  88.2 us
    reduce_scatter x1, waiting for transfers between devices, local(): lax.psum_scatter(shrink_grad.astype(jnp.bfloat16), 'fsdp', scatter_dimens...  88 us
    dynamic_update_slice x4, local copies, waits for them, and re-layouts, back_row(): lax.scan(lambda running, parts: attend_back_block(running, parts, key_hea...  60.6 us
    reduce_scatter x1, waiting for transfers between devices, local(): lax.psum_scatter(inward_grad.astype(jnp.bfloat16), 'fsdp', scatter_dimens...  58 us
    all_gather x1, waiting for transfers between devices, local(): lax.all_gather(shards[0], 'fsdp', axis=0, tiled=True)  46.6 us
    convert_element_type x2, other arithmetic, attend_back_block(): score_back = (probs_full * (prob_back - row_dot)).astype(jnp.bfloat16)  42.8 us
    unnamed x159, local copies, waits for them, and re-layouts  42 us
  transfers between devices with their start and end apart: 9, of which 5 were waited for; matrix products, arithmetic and copies ran while one was open for 21% of the time, Pallas kernels for 0%

commit v1 on v0

v1 whole, which is shorter than its diff:
```python
import functools, math
import jax, jax.numpy as jnp
import numpy as np
from jax import lax
from jax.sharding import PartitionSpec as P
from jax.experimental import pallas as pl
from jax.experimental.pallas import tpu as pltpu

HEAD=64
BF=jnp.bfloat16
F32=jnp.float32
NEG=-1000000000.0
VLIM=60*1024*1024
ROOT_HALF = 0.7071067811865476
INV_ROOT_TAU = 0.3989422804014327

def dot_nn(a,b): return lax.dot_general(a,b,(((1,),(0,)),((),())),preferred_element_type=F32)
def dot_nt(a,b): return lax.dot_general(a,b,(((1,),(1,)),((),())),preferred_element_type=F32)
def dot_tn(a,b): return lax.dot_general(a,b,(((0,),(0,)),((),())),preferred_element_type=F32)

def tables(length):
    lane=np.arange(128)
    freq=10000.0 ** (-2.0*((lane%64)//2)/64)
    ang=np.arange(length)[:,None]*freq[None,:]
    cos=np.cos(ang); sin=np.sin(ang)
    even=(lane%2==0)[None,:]
    return (cos.astype(np.float32), np.where(even,-sin,0).astype(np.float32), np.where(even,0,sin).astype(np.float32))

def rotate(u,cos,up,down):
    return u*cos + pltpu.roll(u,127,1)*up + pltpu.roll(u,1,1)*down

def qkv_kernel(x_ref,w_ref,b_ref,cos_ref,up_ref,down_ref,o_ref):
    x=x_ref[...]
    cos=cos_ref[...]; up=up_ref[...]; down=down_ref[...]
    width=w_ref.shape[1]
    model=x.shape[1]
    for c in range(width//256):
        acc=dot_nn(x,w_ref[:,c*256:(c+1)*256])+b_ref[:,c*256:(c+1)*256]
        for t in range(2):
            lo=c*256+t*128
            u=acc[:,t*128:(t+1)*128]
            if lo<2*model:
                u=rotate(u,cos,up,down)
            if lo<model:
                u=u*0.125
            o_ref[:,lo:lo+128]=u.astype(BF)

def qkv_call(x,w,b,tabs,length,bt=256):
    n,model=x.shape
    per=length//bt
    width=w.shape[1]
    tspec=pl.BlockSpec((bt,128),lambda i:(i%per,0))
    return pl.pallas_call(qkv_kernel,grid=(n//bt,),
        in_specs=[pl.BlockSpec((bt,model),lambda i:(i,0)),
                  pl.BlockSpec((model,width),lambda i:(0,0)),
                  pl.BlockSpec((1,width),lambda i:(0,0)),tspec,tspec,tspec],
        out_specs=pl.BlockSpec((bt,width),lambda i:(i,0)),
        out_shape=jax.ShapeDtypeStruct((n,width),BF),
        cost_estimate=pl.CostEstimate(flops=2*n*model*width,bytes_accessed=2*(n*model+model*width+n*width),transcendentals=0),
        compiler_params=pltpu.CompilerParams(vmem_limit_bytes=VLIM))(x,w,b,*tabs)

def attn_kernel(len_ref,q_ref,k_ref,v_ref,o_ref,qa_ref,*,bq):
    length=q_ref.shape[0]
    live=len_ref[pl.program_id(0)]
    lane=lax.broadcasted_iota(jnp.int32,(length,128),1)
    pos=lax.broadcasted_iota(jnp.int32,(length,128),0)
    k=k_ref[...].astype(F32); v=v_ref[...].astype(F32)
    kh=[];vh=[]
    for h in range(2):
        own=(lane//64)==h
        aux=64*(1-h)
        kh.append(jnp.where(own,k,jnp.where((lane==aux)&(pos>=live),NEG,0.0)).astype(BF))
        vh.append(jnp.where(own,v,1.0).astype(BF))
    lane=lax.broadcasted_iota(jnp.int32,(bq,128),1)
    for i in range(length//bq):
        q=q_ref[i*bq:(i+1)*bq,:].astype(F32)
        parts=[]
        for h in range(2):
            own=(lane//64)==h
            aux=64*(1-h)
            qh=jnp.where(own,q,jnp.where(lane==aux,1.0,0.0)).astype(BF)
            s=dot_nt(qh,kh[h])
            m=jnp.max(s,-1,keepdims=True)
            e=jnp.exp(s-m).astype(BF)
            o=dot_nn(e,vh[h])
            parts.append(o/pltpu.roll(o,64,1))
            neg=-(m+jnp.log(o))
            hi=neg.astype(BF).astype(F32)
            mid=(neg-hi).astype(BF).astype(F32)
            low=neg-hi-mid
            qa=jnp.where(own,q,jnp.where(lane==aux,hi,jnp.where(lane==aux+1,mid,jnp.where(lane==aux+2,low,jnp.where(lane==aux+3,1.0,0.0)))))
            qa_ref[h,i*bq:(i+1)*bq,:]=qa.astype(BF)
        o_ref[i*bq:(i+1)*bq,:]=jnp.where(lane<64,parts[0],parts[1]).astype(BF)

def attn_call(lengths,qkv,length,bq=256):
    n,width=qkv.shape
    rows=n//length
    pairs=width//3//128
    gs=pltpu.PrefetchScalarGridSpec(num_scalar_prefetch=1,grid=(rows,pairs),
        in_specs=[pl.BlockSpec((length,128),lambda b,p,_:(b,p)),
                  pl.BlockSpec((length,128),lambda b,p,_:(b,pairs+p)),
                  pl.BlockSpec((length,128),lambda b,p,_:(b,2*pairs+p))],
        out_specs=[pl.BlockSpec((length,128),lambda b,p,_:(b,p)),
                   pl.BlockSpec((None,2,length,128),lambda b,p,_:(b,p,0,0))])
    return pl.pallas_call(functools.partial(attn_kernel,bq=bq),grid_spec=gs,
        out_shape=[jax.ShapeDtypeStruct((n,width//3),BF),jax.ShapeDtypeStruct((rows,2*pairs,length,128),BF)],
        cost_estimate=pl.CostEstimate(flops=rows*pairs*2*4*length*length*128,bytes_accessed=2*(n*width*2),transcendentals=rows*pairs*2*length*length),
        compiler_params=pltpu.CompilerParams(vmem_limit_bytes=VLIM))(lengths,qkv,qkv,qkv)

def back_kernel(len_ref,qa_ref,k_ref,v_ref,o_ref,do_ref,cos_ref,up_ref,down_ref,dq_ref,dk_ref,dv_ref,doa_ref,dqt_ref,*,bk):
    length=k_ref.shape[0]
    live=len_ref[pl.program_id(0)]
    lane=lax.broadcasted_iota(jnp.int32,(length,128),1)
    do=do_ref[...].astype(F32)
    prod=do*o_ref[...].astype(F32)
    for h in range(2):
        own=(lane//64)==h
        aux=64*(1-h)
        neg=-jnp.sum(jnp.where(own,prod,0.0),-1,keepdims=True)
        hi=neg.astype(BF).astype(F32)
        low=neg-hi
        doa_ref[h]=jnp.where(own,do,jnp.where(lane==aux,hi,jnp.where(lane==aux+1,low,0.0))).astype(BF)
    lane=lax.broadcasted_iota(jnp.int32,(bk,128),1)
    pos=lax.broadcasted_iota(jnp.int32,(bk,128),0)
    for i in range(length//bk):
        sl=slice(i*bk,(i+1)*bk)
        k=k_ref[sl,:].astype(F32); v=v_ref[sl,:].astype(F32)
        kt=k.T.astype(BF)
        dks=[];dvs=[]
        for h in range(2):
            own=(lane//64)==h
            aux=64*(1-h)
            ka=jnp.where(own,k,jnp.where((lane>=aux)&(lane<aux+3),1.0,jnp.where((lane==aux+3)&(pos+i*bk>=live),NEG,0.0))).astype(BF)
            va=jnp.where(own,v,jnp.where((lane==aux)|(lane==aux+1),1.0,0.0)).astype(BF)
            qa=qa_ref[h]
            doa=doa_ref[h]
            p=jnp.exp(dot_nt(ka,qa))
            ds=(p*dot_nt(va,doa)).astype(BF)
            dvs.append(dot_nn(p.astype(BF),doa))
            dks.append(dot_nn(ds,qa))
            t=dot_nn(kt[h*64:(h+1)*64,:],ds)
            if i==0: dqt_ref[h*64:(h+1)*64,:]=t
            else: dqt_ref[h*64:(h+1)*64,:]+=t
        dv_ref[sl,:]=jnp.where(lane<64,dvs[0],dvs[1]).astype(BF)
        dk=jnp.where(lane<64,dks[0],dks[1])
        dk_ref[sl,:]=rotate(dk,cos_ref[sl,:],-up_ref[sl,:],-down_ref[sl,:]).astype(BF)
    dq=dqt_ref[...].T*0.125
    dq_ref[...]=rotate(dq,cos_ref[...],-up_ref[...],-down_ref[...]).astype(BF)

def back_call(lengths,qa,qkv,attn,dattn,tabs,length,bk=256):
    n,width=qkv.shape
    rows=n//length
    pairs=width//3//128
    col=lambda b,p,_:(b,p)
    tspec=pl.BlockSpec((length,128),lambda b,p,_:(0,0))
    gs=pltpu.PrefetchScalarGridSpec(num_scalar_prefetch=1,grid=(rows,pairs),
        in_specs=[pl.BlockSpec((None,2,length,128),lambda b,p,_:(b,p,0,0)),
                  pl.BlockSpec((length,128),lambda b,p,_:(b,pairs+p)),
                  pl.BlockSpec((length,128),lambda b,p,_:(b,2*pairs+p)),
                  pl.BlockSpec((length,128),col),pl.BlockSpec((length,128),col),tspec,tspec,tspec],
        out_specs=[pl.BlockSpec((length,128),col)]*3,
        scratch_shapes=[pltpu.VMEM((2,length,128),BF),pltpu.VMEM((128,length),F32)])
    o=jax.ShapeDtypeStruct((n,width//3),BF)
    return pl.pallas_call(functools.partial(back_kernel,bk=bk),grid_spec=gs,out_shape=[o,o,o],
        cost_estimate=pl.CostEstimate(flops=rows*pairs*2*10*length*length*128,bytes_accessed=2*(n*width*3),transcendentals=rows*pairs*2*length*length),
        compiler_params=pltpu.CompilerParams(vmem_limit_bytes=VLIM))(lengths,qa,qkv,qkv,attn,dattn,*tabs)

def norm_fwd(u):
    c=u-jnp.mean(u,-1,keepdims=True)
    r=lax.rsqrt(jnp.mean(c*c,-1,keepdims=True)+1e-12)
    return c*r,r
def norm_bwd(gy,n,r,g):
    a=gy*g
    return r*(a-jnp.mean(a,-1,keepdims=True)-n*jnp.mean(a*n,-1,keepdims=True))

def ffn_kernel(len_ref,x_ref,at_ref,cot_ref,wo_ref,w1_ref,w2_ref,v_ref,
               out_ref,act_ref,dz_ref,y1_ref,dpre_ref,dr1_ref,da_ref,dat_ref,dvec_ref,slope_ref,*,length,fc):
    step=pl.program_id(0)
    bt,model=x_ref.shape
    ff=w1_ref.shape[1]
    per=length//bt
    live=len_ref[step//per]
    row=lambda i:v_ref[i:i+1,:]
    r1=x_ref[...].astype(F32)+(dot_nn(at_ref[...],wo_ref[...])+row(7))
    n1,i1=norm_fwd(r1)
    y1=n1*row(0)+row(2)
    y1b=y1.astype(BF)
    y1_ref[...]=y1b
    z=jnp.zeros((bt,model),F32)
    for c in range(ff//fc):
        sl=slice(c*fc,(c+1)*fc)
        bias=v_ref[9+c*fc//model:10+c*fc//model,(c*fc)%model:(c*fc)%model+fc]
        pre=dot_nn(y1b,w1_ref[:,sl])+bias
        phi=0.5*(1.0+lax.erf(pre*ROOT_HALF))
        act=(pre*phi).astype(BF)
        act_ref[:,sl]=act
        slope_ref[:,sl]=phi+pre*(jnp.exp(-0.5*pre*pre)*INV_ROOT_TAU)
        z=z+dot_nn(act,w2_ref[sl,:])
    r2=y1+(z+row(8))
    n2,i2=norm_fwd(r2)
    out_ref[...]=(n2*row(1)+row(3)).astype(BF)
    pos=lax.broadcasted_iota(jnp.int32,(bt,model),0)+(step%per)*bt
    e=jnp.where(pos<live,cot_ref[...].astype(F32),0.0)
    dr2=norm_bwd(e,n2,i2,row(1))
    dz=dr2.astype(BF)
    dz_ref[...]=dz
    @pl.when(step==0)
    def _():
        dvec_ref[...]=jnp.zeros_like(dvec_ref)
    def add(i,val,off=0):
        dvec_ref[i:i+1,off:off+val.shape[1]]+=jnp.sum(val,0,keepdims=True)
    add(1,e*n2); add(3,e); add(8,dz.astype(F32))
    dy=dr2
    for c in range(ff//fc):
        sl=slice(c*fc,(c+1)*fc)
        dpre=(dot_nt(dz,w2_ref[sl,:])*slope_ref[:,sl]).astype(BF)
        dpre_ref[:,sl]=dpre
        add(9+c*fc//model,dpre.astype(F32),(c*fc)%model)
        dy=dy+dot_nt(dpre,w1_ref[:,sl])
    add(0,dy*n1); add(2,dy)
    dr1=norm_bwd(dy,n1,i1,row(0))
    dr1_ref[...]=dr1
    da=dr1.astype(BF)
    da_ref[...]=da
    add(7,da.astype(F32))
    dat_ref[...]=dot_nt(da,wo_ref[...]).astype(BF)

def ffn_call(lengths,x,at,cot,wo,w1,w2,vec,length,bt=256,fc=768):
    n,model=x.shape
    ff=w1.shape[1]
    tok=pl.BlockSpec((bt,model),lambda i,_:(i,0))
    wide=pl.BlockSpec((bt,ff),lambda i,_:(i,0))
    full=lambda a:pl.BlockSpec(a.shape,lambda i,_:(0,0),pipeline_mode=pl.Buffered(1))
    gs=pltpu.PrefetchScalarGridSpec(num_scalar_prefetch=1,grid=(n//bt,),
        in_specs=[tok,tok,tok,full(wo),full(w1),full(w2),full(vec)],
        out_specs=[tok,wide,tok,tok,wide,tok,tok,tok,pl.BlockSpec((13,model),lambda i,_:(0,0))],
        scratch_shapes=[pltpu.VMEM((bt,ff),F32)])
    s=lambda w,t:jax.ShapeDtypeStruct((n,w),t)
    return pl.pallas_call(functools.partial(ffn_kernel,length=length,fc=fc),grid_spec=gs,
        out_shape=[s(model,BF),s(ff,BF),s(model,BF),s(model,BF),s(ff,BF),s(model,F32),s(model,BF),s(model,BF),jax.ShapeDtypeStruct((13,model),F32)],
        cost_estimate=pl.CostEstimate(flops=n*(4*model*model+8*model*ff),bytes_accessed=n*(model*20+ff*4)+model*ff*4,transcendentals=n*ff*2),
        compiler_params=pltpu.CompilerParams(vmem_limit_bytes=VLIM))(lengths,x,at,cot,wo,w1,w2,vec)

STEP=10
BETA_ONE=0.5
BETA_TWO=0.5
ADAM_EPS=1e-08
WEIGHT_DECAY=0.01
OUT_FAN=3


def adam_update(master, moment, square, gradient, rate, decay):
    momentum = BETA_ONE * moment + (1.0 - BETA_ONE) * gradient
    squares = BETA_TWO * square + (1.0 - BETA_TWO) * gradient * gradient
    corrected = momentum / (1.0 - BETA_ONE**STEP)
    spread = jnp.sqrt(squares / (1.0 - BETA_TWO**STEP))
    return (master - rate * (corrected / (spread + ADAM_EPS) + decay * master), momentum, squares)


def local(tokens,cotangent,lengths,inward_weight,inward_moment,inward_square,outward_weight,outward_moment,outward_square,
          expand_weight,expand_moment,expand_square,shrink_weight,shrink_moment,shrink_square,vectors,vector_moment,vector_square):
    rows,length,model=tokens.shape
    x=tokens.reshape(-1,model)
    cot=cotangent.reshape(-1,model)
    t=[jnp.asarray(a) for a in tables(length)]
    gather=lambda w,axis=0: lax.all_gather(w.astype(BF),"fsdp",axis=axis,tiled=True)
    wqkv=gather(inward_weight)
    vec=gather(vectors,1).astype(F32)
    wo=gather(outward_weight)
    w1=gather(expand_weight)
    w2=gather(shrink_weight)
    qkv=qkv_call(x,wqkv,vec[4:7].reshape(1,-1),t,length)
    attn,qa=attn_call(lengths,qkv,length)
    out,act,dz,y1,dpre,dr1,da,dat,dvec=ffn_call(lengths,x,attn,cot,wo,w1,w2,vec,length)
    dw2=dot_tn(act,dz).astype(BF)
    dw1=dot_tn(y1,dpre).astype(BF)
    dwo=dot_tn(attn,da).astype(BF)
    dq,dk,dv=back_call(lengths,qa,qkv,attn,dat,t,length)
    dwq=jnp.concatenate([dot_tn(x,g).astype(BF) for g in (dq,dk,dv)],1)
    tg=(dr1+dot_nt(dq,wqkv[:,:model])+dot_nt(dk,wqkv[:,model:2*model])+dot_nt(dv,wqkv[:,2*model:])).astype(BF)
    db=[jnp.sum(g,0,dtype=F32)[None] for g in (dq,dk,dv)]
    dvec=jnp.concatenate([dvec[:4],*db,dvec[7:]])
    def reduce(g,axis=0):
        r=lax.psum_scatter(g,"fsdp",scatter_dimension=axis,tiled=True)
        return lax.psum(r.astype(F32),"dp")
    new=[]
    for w,m,s,g,rate,decay in ((inward_weight,inward_moment,inward_square,reduce(dwq),1/math.sqrt(model),WEIGHT_DECAY),
                    (outward_weight,outward_moment,outward_square,reduce(dwo),1/math.sqrt(OUT_FAN),WEIGHT_DECAY),
                    (expand_weight,expand_moment,expand_square,reduce(dw1),1/math.sqrt(model),WEIGHT_DECAY),
                    (shrink_weight,shrink_moment,shrink_square,reduce(dw2),1/math.sqrt(w1.shape[1]),WEIGHT_DECAY),
                    (vectors,vector_moment,vector_square,reduce(dvec,1),0.5,0.0)):
        new+=list(adam_update(w,m,s,g,rate,decay))
    return (out.reshape(tokens.shape),tg.reshape(tokens.shape),*new)


def solution(mesh):
    in_specs = (
        P(("dp", "fsdp"), None, None),
        P(("dp", "fsdp"), None, None),
        P(("dp", "fsdp")),
        P("fsdp", None),
        P("fsdp", None),
        P("fsdp", None),
        P("fsdp", None),
        P("fsdp", None),
        P("fsdp", None),
        P("fsdp", None),
        P("fsdp", None),
        P("fsdp", None),
        P("fsdp", None),
        P("fsdp", None),
        P("fsdp", None),
        P(None, "fsdp"),
        P(None, "fsdp"),
        P(None, "fsdp"),
    )
    out_specs = (
        P(("dp", "fsdp"), None, None),
        P(("dp", "fsdp"), None, None),
        P("fsdp", None),
        P("fsdp", None),
        P("fsdp", None),
        P("fsdp", None),
        P("fsdp", None),
        P("fsdp", None),
        P("fsdp", None),
        P("fsdp", None),
        P("fsdp", None),
        P("fsdp", None),
        P("fsdp", None),
        P("fsdp", None),
        P(None, "fsdp"),
        P(None, "fsdp"),
        P(None, "fsdp"),
    )
    return jax.shard_map(local, mesh=mesh, in_specs=in_specs, out_specs=out_specs, check_vma=False)
```

time: 1100 us -> 851 us (0.77)
  matrix products: 297 us -> 36.6 us
  waiting for transfers between devices: 321 us -> 474 us
  local copies, waits for them, and re-layouts: 151 us -> 15.6 us
  Pallas kernels: 0 us -> 113 us
  other arithmetic: 139 us -> 30.1 us
    dot_general x26 -> x9, matrix products: 297 us -> 36.6 us  [the longest x6 29.7 us: dot_tn(): lax.dot_general(a, b, (((0,), (0,)), ((), ())), preferred_element_type=F32)]
    all_gather x4, waiting for transfers between devices: 87.1 us -> 229 us  [local(): lax.all_gather(w.astype(BF), 'fsdp', axis=axis, tiled=True)]
    pallas_call x0 -> x4, Pallas kernels: none -> 113 us  [the longest x1 39.5 us: back_call(): pl.pallas_call(functools.partial(back_kernel, bk=bk), grid_spec=gs, out_s...]
    dynamic_update_slice x4 -> x0, local copies, waits for them, and re-layouts: 60.6 us -> none  [back_row(): lax.scan(lambda running, parts: attend_back_block(running, parts, key_hea...]
    convert_element_type x8 -> x4, other arithmetic: 66.4 us -> 7.34 us  [local(): w.astype(BF)]
    unnamed x159 -> x57, local copies, waits for them, and re-layouts: 42 us -> 13.8 us
    reduce_sum x9 -> x2, other arithmetic: 31.6 us -> 3.7 us  [local(): db = [jnp.sum(g, 0, dtype=F32)[None] for g in (dq, dk, dv)]]
    another operation x5 -> x0, other arithmetic: 20.5 us -> none
  transfers between devices with their start and end apart: 9 -> 9, of which waited for: 5 -> 7; matrix products, arithmetic and copies ran while one was open for 21% -> 6% of each run, Pallas kernels for 0% -> 4%
where the time goes in v1:
time: 851 us; the launch traced here: 845 us
  waiting for transfers between devices  474 us (56%)
  blocking collectives  160 us (19%)
  Pallas kernels  113 us (13%)
  matrix products  36.6 us (4%)
  other arithmetic  30.1 us (4%)
  local copies, waits for them, and re-layouts  15.6 us (2%)
  between operations  15.1 us (2%)
    reduce_scatter x4, waiting for transfers between devices, reduce(): r = lax.psum_scatter(g, 'fsdp', scatter_dimension=axis, tiled=True)  245 us
    all_gather x4, waiting for transfers between devices, local(): lax.all_gather(w.astype(BF), 'fsdp', axis=axis, tiled=True)  229 us
    psum x1, blocking collectives, reduce(): return lax.psum(r.astype(F32), 'dp')  145 us
    pallas_call x1, Pallas kernels, back_call(): pl.pallas_call(functools.partial(back_kernel, bk=bk), grid_spec=gs, out_s...  39.5 us
    pallas_call x1, Pallas kernels, ffn_call(): pl.pallas_call(functools.partial(ffn_kernel, length=length, fc=fc), grid_...  38.8 us
    dot_general x6, matrix products, dot_tn(): lax.dot_general(a, b, (((0,), (0,)), ((), ())), preferred_element_type=F32)  29.7 us
    pallas_call x1, Pallas kernels, attn_call(): pl.pallas_call(functools.partial(attn_kernel, bq=bq), grid_spec=gs, out_s...  26.6 us
    sub x5, other arithmetic, adam_update(): master - rate * (corrected / (spread + ADAM_EPS) + decay * master)  18.7 us
  transfers between devices with their start and end apart: 9, of which 7 were waited for; matrix products, arithmetic and copies ran while one was open for 6% of the time, Pallas kernels for 4%

profile of v1, /device:TPU:0, one launch (start us, length us, event | category | flops | bytes accessed | tf_op | source)
XLA Modules:
  0.0 845.4 jit_solution(16230488875397002777)
XLA Ops:
  7.3 2.6 convert_element_type.69
  10.0 0.7 convert_element_type.72
  10.8 1.2 convert_element_type.73
  12.1 2.8 convert_element_type.74
  15.6 15.0 %all-gather = bf16[4,192,13]{1,2,0:T(8,128)(2,1)S(1)} all-gather(bf16[1,192,13]{1,2,0:T(8,128)(2,1)S(1)} %convert_bitcast_fusion), channel_id=1, replica_groups=mesh['dp'=8,'fsdp'=4] {'fsdp'}, dimensions={0}, use_global_device_ids=true | all-gather | bytes 24960 | tf_op jit(solution)/shard_map/all_gather | solution.py:266
  30.7 0.6 copy.60
  31.3 51.9 %all-gather.6.cloned.1.call-done.w_ref = bf16[768,2304]{1,0:T(8,128)(2,1)} async-done(((bf16[192,2304]{1,0:T(8,128)(2,1)}), bf16[768,2304]{1,0:T(8,128)(2,1)}) %all-gather.6.cloned.1.call-update) | async-done | bytes 3538960 | tf_op jit(solution)/shard_map/all_gather | solution.py:266
  83.2 8.5 %shard_map.332.q_ref.k_ref.v_ref = bf16[1024,2304]{1,0:T(8,128)(2,1)} custom-call(bf16[1024,768]{1,0:T(8,128)(2,1)} %bitcast.49, bf16[768,2304]{1,0:T(8,128)(2,1)} %all-gather.6.cloned.1.call-done.w_ref, f32[1,2304]{1,0:T(1,128)} %bitcast.47, f32[1024,128]{1,0:T(8,128)} %constant.21.clone.cos_ref, f32[1024,128]{1,0:T(8,128)} %constant.22.clone.up_ref, ...), custom_call_target="tpu_custom_call" | custom-call | flops 3623878656 | bytes 9830400 | tf_op jit(solution)/shard_map/pallas_call | solution.py:53
  91.6 26.6 %shard_map.333 = (bf16[1024,768]{1,0:T(8,128)(2,1)}, bf16[1,12,1024,128]{3,2,1,0:T(8,128)(2,1)}) custom-call(s32[1]{0:T(128)S(6)} %copy.70.len_ref, bf16[1024,2304]{1,0:T(8,128)(2,1)} %shard_map.332.q_ref.k_ref.v_ref, bf16[1024,2304]{1,0:T(8,128)(2,1)} %shard_map.332.q_ref.k_ref.v_ref, bf16[1024,2304]{1,0:T(8,128)(2,1)} %shard_map.332.q_ref.k_ref.v_ref), custom_call_target="tpu_custom_call" | custom-call | flops 6442450944 | bytes 9437184 | tf_op jit(solution)/shard_map/pallas_call | solution.py:105
  118.2 86.9 %all-gather.10.cloned.1.call-done.w1_ref = bf16[768,3072]{1,0:T(8,128)(2,1)} async-done(((bf16[192,3072]{1,0:T(8,128)(2,1)}), bf16[768,3072]{1,0:T(8,128)(2,1)}) %all-gather.10.cloned.1.call-update) | async-done | bytes 4718608 | tf_op jit(solution)/shard_map/all_gather | solution.py:266
  205.1 89.9 %all-gather.12.cloned.1.call-done.w2_ref = bf16[3072,768]{1,0:T(8,128)(2,1)} async-done(((bf16[768,768]{1,0:T(8,128)(2,1)}), bf16[3072,768]{1,0:T(8,128)(2,1)}) %all-gather.12.cloned.1.call-update) | async-done | bytes 4718608 | tf_op jit(solution)/shard_map/all_gather | solution.py:266
  295.0 38.8 %shard_map.334 = (bf16[1024,768]{1,0:T(8,128)(2,1)}, bf16[1024,3072]{1,0:T(8,128)(2,1)}, bf16[1024,768]{1,0:T(8,128)(2,1)}, bf16[1024,768]{1,0:T(8,128)(2,1)}, b...) custom-call(s32[1]{0:T(128)S(6)} %copy.70.len_ref, ...), custom_call_target="tpu_custom_call" | custom-call | flops 21743271936 | bytes 37748736 | tf_op jit(solution)/shard_map/pallas_call | solution.py:239
  333.8 0.7 slice.22
  334.6 0.8 slice.23
  335.4 39.5 %shard_map.335 = (bf16[1024,768]{1,0:T(8,128)(2,1)}, bf16[1024,768]{1,0:T(8,128)(2,1)}, bf16[1024,768]{1,0:T(8,128)(2,1)}) custom-call(s32[1]{0:T(128)S(6)} %copy.70.len_ref, bf16[1,12,1024,128]{3,2,1,0:T(8,128)(2,1)} %get-tuple-element.34.qa_ref, bf16[1024,2304]{1,0:T(8,128)(2,1)} %shard_map.332.q_ref.k_ref.v_ref, ...), custom_call_target="tpu_custom_call" | custom-call | flops 16106127360 | bytes 14155776 | tf_op jit(solution)/shard_map/pallas_call | solution.py:164
  374.9 1.8 convert_reduce_fusion.2
  376.8 1.9 convert_reduce_fusion
  378.9 0.9 copy.58
  379.9 4.5 convolution_convert_fusion.2
  384.4 0.3 reduce-scatter.16.cloned.1.call-start
  384.6 3.0 fusion.4
  387.7 1.5 fusion.5
  389.1 1.5 fusion.6
  390.6 0.4 pad_maximum_fusion
  391.0 4.0 copy.56
  395.1 1.3 copy-done.24
  396.4 9.5 %convolution_convert_fusion.1 = bf16[768,3072]{1,0:T(8,128)(2,1)} fusion(bf16[1024,768]{1,0:T(8,128)(2,1)S(1)} %copy-done.24, bf16[1024,3072]{1,0:T(8,128)(2,1)} %get-tuple-element.41), kind=kOutput, calls=%fused_computation.1 | convolution fusion | flops 4834197504 | bytes 12582912 | tf_op jit(solution)/shard_map/dot_general | solution.py:19
  406.0 0.3 reduce-scatter.14.cloned.1.call-start
  406.3 1.1 copy-done.25
  407.4 9.8 %convolution_convert_fusion = bf16[3072,768]{1,0:T(8,128)(2,1)} fusion(bf16[1024,3072]{1,0:T(8,128)(2,1)} %get-tuple-element.42, bf16[1024,768]{1,0:T(8,128)(2,1)S(1)} %copy-done.25), kind=kOutput, calls=%fused_computation | convolution fusion | flops 4834197504 | bytes 12582912 | tf_op jit(solution)/shard_map/dot_general | solution.py:19
  417.3 1.4 copy-done.18
  418.6 2.8 fusion.8
  421.5 1.4 fusion.10
  423.0 0.9 copy-done.6
  423.9 2.6 fusion.3
  426.5 1.1 copy.59
  427.6 1.8 reduce-scatter.10.cloned.1.call-done
  429.3 67.5 %reduce-scatter.16.cloned.1.call-done = bf16[192,2304]{1,0:T(8,128)(2,1)} async-done(((bf16[768,2304]{1,0:T(8,128)(2,1)}), bf16[192,2304]{1,0:T(8,128)(2,1)}) %reduce-scatter.16.cloned.1.call-update) | async-done | bytes 884752 | tf_op jit(solution)/shard_map/reduce_scatter | solution.py:284
  496.9 88.0 %reduce-scatter.12.cloned.1.call-done = bf16[192,3072]{1,0:T(8,128)(2,1)} async-done(((bf16[768,3072]{1,0:T(8,128)(2,1)}), bf16[192,3072]{1,0:T(8,128)(2,1)}) %reduce-scatter.12.cloned.1.call-update) | async-done | bytes 1179664 | tf_op jit(solution)/shard_map/reduce_scatter | solution.py:284
  584.9 88.2 %reduce-scatter.14.cloned.1.call-done = bf16[768,768]{1,0:T(8,128)(2,1)} async-done(((bf16[3072,768]{1,0:T(8,128)(2,1)}), bf16[768,768]{1,0:T(8,128)(2,1)}) %reduce-scatter.14.cloned.1.call-update) | async-done | bytes 1179664 | tf_op jit(solution)/shard_map/reduce_scatter | solution.py:284
  673.1 144.6 %all-reduce.2 = (f32[192,2304]{1,0:T(8,128)}, f32[192,768]{1,0:T(8,128)}, f32[192,3072]{1,0:T(8,128)}, f32[768,768]{1,0:T(8,128)S(1)}, f32[13,192]{1,0:T(8,128)}) all-reduce(bf16[192,2304]{1,0:T(8,128)(2,1)} %reduce-scatter.16.cloned.1.call-done, ...), channel_id=1, replica_groups=mesh['dp'=8,'fsdp'=4] {'dp'}, use_global_device_ids=true, to_apply=%region_1.0 | all-reduce | flops 1771968 | bytes 10636800 | tf_op jit(solution)/shard_map/psum | solution.py:285
  817.6 1.5 multiply_subtract_fusion.4
  819.2 2.7 multiply_subtract_fusion.3
  822.0 5.5 multiply_subtract_fusion.2
  827.5 1.2 copy-done.13
  828.7 4.6 multiply_subtract_fusion.1
  833.3 1.0 copy-done.12
  834.3 4.2 multiply_subtract_fusion
  (72 shorter events, 0.9 us)
Async XLA Ops:
  7.2 2.8 copy-start.7
  7.2 3.6 copy-start
  7.2 76.0 %all-gather.6.cloned.1.call-start = ((), (), s32[]{:S(2)}) async-start(), calls=%async_computation.5 | async-start | bytes 4423680 | tf_op jit(solution)/shard_map/all_gather | solution.py:266
  9.9 108.3 %all-gather.8.cloned.1.call-start = ((), (), s32[]{:S(2)}) async-start(), calls=%async_computation.6 | async-start | bytes 1474560 | tf_op jit(solution)/shard_map/all_gather | solution.py:266
  10.7 194.4 %all-gather.10.cloned.1.call-start = ((), (), s32[]{:S(2)}) async-start(), calls=%async_computation.7 | async-start | bytes 5898240 | tf_op jit(solution)/shard_map/all_gather | solution.py:266
  12.0 3.6 copy-start.22
  12.0 283.0 %all-gather.12.cloned.1.call-start = ((), (), s32[]{:S(2)}) async-start(), calls=%async_computation.8 | async-start | bytes 5898240 | tf_op jit(solution)/shard_map/all_gather | solution.py:266
  14.9 411.6 %reduce-scatter.18.cloned.1.call-start = ((), (), s32[]{:S(2)}) async-start(), calls=%async_computation.13 | async-start | bytes 491520
  30.7 61.0 %copy-start.21 = (f32[768,13]{0,1:T(8,128)}, f32[768,13]{0,1:T(8,128)S(1)}, u32[]{:S(2)}) copy-start(f32[768,13]{0,1:T(8,128)S(1)} %reshape.56) | copy-start | bytes 119812
  374.9 1.9 copy-start.4
  379.8 49.5 %reduce-scatter.10.cloned.1.call-start = ((), (), s32[]{:S(2)}) async-start(), calls=%async_computation.9 | async-start | bytes 1474560 | tf_op jit(solution)/shard_map/reduce_scatter | solution.py:284
  379.9 4.8 copy-start.15
  384.4 112.5 %reduce-scatter.16.cloned.1.call-start = ((), (), s32[]{:S(2)}) async-start(), calls=%async_computation.12 | async-start | bytes 4423680 | tf_op jit(solution)/shard_map/reduce_scatter | solution.py:284
  384.6 3.0 copy-start.17
  384.6 3.0 copy-start.23
  395.0 1.4 copy-start.24
  395.1 189.8 %reduce-scatter.12.cloned.1.call-start = ((), (), s32[]{:S(2)}) async-start(), calls=%async_computation.10 | async-start | bytes 5898240 | tf_op jit(solution)/shard_map/reduce_scatter | solution.py:284
  406.0 1.4 copy-start.25
  406.0 267.1 %reduce-scatter.14.cloned.1.call-start = ((), (), s32[]{:S(2)}) async-start(), calls=%async_computation.11 | async-start | bytes 5898240 | tf_op jit(solution)/shard_map/reduce_scatter | solution.py:284
  417.2 1.4 copy-start.18
  418.6 2.9 copy-start.16
  418.6 2.9 copy-start.20
  421.5 1.4 copy-start.5
  421.5 2.4 copy-start.6
  426.5 392.7 %copy-start.8 = (f32[192,768]{1,0:T(8,128)S(1)}, f32[192,768]{1,0:T(8,128)}, u32[]{:S(2)}) copy-start(f32[192,768]{1,0:T(8,128)} %param.27) | copy-start | bytes 1769476
  426.5 392.7 %copy-start.19 = (f32[192,768]{1,0:T(8,128)S(1)}, f32[192,768]{1,0:T(8,128)}, u32[]{:S(2)}) copy-start(f32[192,768]{1,0:T(8,128)} %param.28) | copy-start | bytes 1769476
  817.6 4.3 copy-start.3
  817.6 4.3 copy-start.14
  821.9 5.6 copy-start.1
  821.9 5.6 copy-start.9
  822.0 5.5 copy-start.10
  822.0 6.7 copy-start.13
  828.7 4.6 copy-start.2
  828.7 4.6 copy-start.11
  828.7 5.6 copy-start.12
Sparse Core Ops, SparseCore 0:
  10.2 72.9 all-gather.5
  85.3 29.0 all-gather.7
  116.5 88.5 all-gather.9
  207.1 87.8 all-gather.11
  379.9 19.0 reduce-scatter.17
  401.9 27.4 reduce-scatter.9
  431.8 65.0 reduce-scatter.15
  499.3 85.5 reduce-scatter.11
  587.3 85.7 reduce-scatter.13
